TPU v7x, 256 devices: a whole 4x4x8 slice. The times are simulated.
256 devices in a mesh: tile: 32 (over x, z), pair: 8 (over y, core).
Axes of the slice: x: 4, y: 4, z: 8, core: 2. Of those that a mesh axis runs over, the one named last changes fastest.
Arguments:
- amplitudes: bfloat16 [128, 96, 512], P('pair', 'tile'), may hold values from -6 to 6
- tasks: int32 [6144, 2], P(('tile', 'pair')), may hold values from 0 to 95, as said below
- integrals: bfloat16 [6144, 512, 512], P(('tile', 'pair')), may hold values from -0.0625 to 0.0625
Outputs:
- residual: float32 [128, 96, 512], P('pair', 'tile')
Inputs may be any that keep to these rules, and one draw needn't show every extreme that they name: Each row (a, c) of tasks names two tiles with a % 24 == c % 24 (so of one irrep, a % 8 == c % 8) held by different indices of tile, a // 3 != c // 3. Among the distinct tiles named by the rows of one device (aligned blocks of 24 rows, devices in the order tile, pair), at most one lies in any aligned block of 3 consecutive tiles (the tiles of one owner along tile); every device names exactly one of tiles 0, 1, 2.
All inputs are finite; a program needn't handle non-finite values.
Results may differ from a plain program's by a relative error of at most 0.0003.
Values may be sent and summed in bfloat16 or wider, within the bound.
No kernel may reach another device: no remote copies, remote signals or barrier semaphores. Data moves between devices by JAX's collectives and lax.ppermute only.
A program may use at most 128 MiB of HBM per device.

v0:
```python
import functools

import jax
import jax.numpy as jnp
from jax import lax
from jax.experimental import pallas as pl
from jax.experimental.pallas import tpu as pltpu
from jax.sharding import Mesh
from jax.sharding import PartitionSpec as P

XS, ZS, YS, CORES = 4, 8, 4, 2
PLANE = ("x", "y", "core")
WHOLE = ("x", "z", "y", "core")
PER_STEP = 8
LIMIT = 32

LANES = 128
FULL = 32767.0
STEPS = 256.0
FLOOR = 2.0**-110
MIB = 1024 * 1024
VMEM = pl.BlockSpec(memory_space=pltpu.VMEM)
SMEM = pl.BlockSpec(memory_space=pltpu.SMEM)


def swap(value, axes):
    return lax.all_to_all(value, axes, split_axis=0, concat_axis=0, tiled=True)


def exponents_of(largest):
    return jnp.ceil(jnp.log2(jnp.maximum(largest, FLOOR)) * STEPS)


def exponent_codes(exponents):
    return exponents.astype(jnp.int32).astype(jnp.int16)


def numbers(codes):
    return codes.astype(jnp.int32).astype(jnp.float32)


def scales_of(codes):
    return jnp.exp2(numbers(codes) * (1.0 / STEPS)) * (1.0 / FULL)


def call(kernel, out_shape, in_specs, scratch=()):
    return pl.pallas_call(
        kernel,
        out_shape=out_shape,
        in_specs=in_specs,
        out_specs=jax.tree.map(lambda _: VMEM, out_shape),
        scratch_shapes=scratch,
        compiler_params=pltpu.CompilerParams(vmem_limit_bytes=24 * MIB),
    )


def device(x, z, y, core):
    return ((x % XS * ZS + z) * YS + y % YS) * CORES + core


def move(value, by, near, cross=0):
    table = []
    for x in range(XS):
        for z in range(ZS):
            for y in range(YS):
                for core in range(CORES):
                    along_x = (core == 0) == near
                    to = device(x + by * along_x, z, y + by * (not along_x), core ^ cross)
                    table.append((device(x, z, y, core), to))
    return lax.ppermute(value, WHOLE, table)


def trade(value):
    return lax.ppermute(value, "core", [(0, 1), (1, 0)])


def extra(count, rows):
    return -(-count // rows)


def encode(block_of, count, out, largest_ref, place=()):
    rows = out.shape[-2]
    for at in range(count):
        largest_ref[at : at + 1] = jnp.max(jnp.abs(block_of(at)), axis=0, keepdims=True)
    if count % rows:
        largest_ref[count:] = jnp.zeros_like(largest_ref[count:])
    exponents = exponents_of(largest_ref[...])
    largest_ref[...] = jnp.exp2(exponents * (-1.0 / STEPS)) * FULL
    for at in range(count):
        codes = jnp.round(block_of(at) * largest_ref[at : at + 1])
        out[*place, at] = codes.astype(jnp.int32).astype(jnp.int16)
    for at in range(extra(count, rows)):
        out[*place, count + at] = exponent_codes(exponents[at * rows : (at + 1) * rows])


def scale_blocks(piece, count, place=()):
    rows = piece.shape[-2]
    blocks = [scales_of(piece[*place, count + at]) for at in range(extra(count, rows))]
    return [blocks[at // rows][at % rows : at % rows + 1] for at in range(count)]


def pack_kernel(place_ref, want_ref, *refs):
    gathered, outs = refs[:XS], refs[XS:]
    core = place_ref[2]
    for side in range(CORES):
        for far in range(XS):
            row = far * CORES + side
            for near in range(XS):
                slot = (near + core * (far - near)) * ZS
                for z in range(ZS):
                    outs[side * XS + far][near * ZS + z] = gathered[near][z, want_ref[row, slot + z]]


def spot(place_ref, side, far, near, part):
    core = place_ref[2] ^ side
    slot = pl.multiple_of((near + core * (far - near)) * ZS, ZS)
    return slot, pl.multiple_of((far + core * (near - far)) * part, part)


def lay_out(place_ref, side, pieces, amp):
    part = pieces[0].shape[1]
    for far, piece in enumerate(pieces):
        for near in range(XS):
            slot, row = spot(place_ref, side, far, near, part)
            amp[pl.ds(slot, ZS), pl.ds(row, part)] = piece[near * ZS : (near + 1) * ZS]


def begin_kernel(slot_ref, place_ref, *refs):
    pieces, (across_ref, along_ref, total, amp) = refs[:XS], refs[XS:]
    step = pl.program_id(0)
    half = amp.shape[2]

    @pl.when(step == 0)
    def _():
        lay_out(place_ref, 0, pieces, amp)
        total[...] = jnp.zeros_like(total)

    for at in range(along_ref.shape[0]):
        task = step * along_ref.shape[0] + at
        first = slot_ref[2 * task]
        second = slot_ref[2 * task + 1]
        term = lax.dot_general(
            amp[second], across_ref[at], (((1,), (1,)), ((), ())), preferred_element_type=jnp.float32
        )
        total[0, first] += term[:, :half]
        total[1, first] += term[:, half:]
        term = jnp.dot(amp[first], along_ref[at], preferred_element_type=jnp.float32)
        total[0, second] += term[:, :half]
        total[1, second] += term[:, half:]


def end_kernel(side, slot_ref, place_ref, *refs):
    pieces, (begun, first_ref, second_ref), refs = refs[:XS], refs[XS : XS + 3], refs[XS + 3 :]
    outs, (amp, total, largest) = refs[:XS], refs[XS:]
    step = pl.program_id(0)
    slots, rows, half = total.shape
    part = rows // YS
    chunks = half // LANES

    @pl.when(step == 0)
    def _():
        lay_out(place_ref, 1, pieces, amp)
        total[...] = begun[place_ref[2] ^ side]

    for at in range(first_ref.shape[0]):
        task = step * first_ref.shape[0] + at
        first = slot_ref[2 * task]
        second = slot_ref[2 * task + 1]
        total[first] += lax.dot_general(
            amp[second], first_ref[at], (((1,), (1,)), ((), ())), preferred_element_type=jnp.float32
        )
        total[second] += jnp.dot(amp[first], second_ref[at], preferred_element_type=jnp.float32)

    @pl.when(step == pl.num_programs(0) - 1)
    def _():
        for far in range(XS):
            spots = [spot(place_ref, side, far, near, part) for near in range(XS)]

            def block_of(block):
                entry, lanes = block // chunks, block % chunks * LANES
                slot, row = spots[entry // ZS]
                return total[slot + entry % ZS, pl.ds(row, part), lanes : lanes + LANES]

            encode(block_of, slots * chunks, outs[far], largest.at[far])


def products(kernel, slots, place, operands, blocks, specs, out_shape, scratch, share):
    tasks, width, _ = blocks.shape
    return pl.pallas_call(
        kernel,
        out_shape=out_shape,
        grid_spec=pltpu.PrefetchScalarGridSpec(
            num_scalar_prefetch=2,
            grid=(tasks // PER_STEP,),
            in_specs=[VMEM] * len(operands) + specs,
            out_specs=jax.tree.map(lambda _: VMEM, out_shape),
            scratch_shapes=scratch,
        ),
        compiler_params=pltpu.CompilerParams(vmem_limit_bytes=LIMIT * MIB),
        cost_estimate=pl.CostEstimate(
            flops=4 * tasks * 128 * width * width // share,
            bytes_accessed=4 * tasks * width * width // share,
            transcendentals=0,
        ),
    )(slots, place, *operands, blocks, blocks)


def begin(slots, place, pieces, blocks):
    entries, part, half = pieces[0].shape
    width = blocks.shape[1]
    specs = [
        pl.BlockSpec((PER_STEP, width, half), lambda t, _, place: (t, 0, place[2])),
        pl.BlockSpec((PER_STEP, half, width), lambda t, _, place: (t, place[2], 0)),
    ]
    out = jax.ShapeDtypeStruct((CORES, entries, YS * part, half), jnp.float32)
    scratch = [pltpu.VMEM((entries, YS * part, half), blocks.dtype)]
    return products(begin_kernel, slots, place, pieces, blocks, specs, out, scratch, 2)


def end(side, slots, place, pieces, begun, blocks):
    entries, part, half = pieces[0].shape
    specs = [
        pl.BlockSpec((PER_STEP, half, half), lambda t, _, place: (t, place[2] ^ side, 1 - place[2])),
        pl.BlockSpec((PER_STEP, half, half), lambda t, _, place: (t, 1 - place[2], place[2] ^ side)),
    ]
    count = entries * (half // LANES)
    out = jax.ShapeDtypeStruct((count + extra(count, part), part, LANES), jnp.int16)
    scratch = [
        pltpu.VMEM((entries, YS * part, half), blocks.dtype),
        pltpu.VMEM((entries, YS * part, half), jnp.float32),
        pltpu.VMEM((XS, extra(count, part) * part, LANES), jnp.float32),
    ]
    operands = [*pieces, begun]
    kernel = functools.partial(end_kernel, side)
    return products(kernel, slots, place, operands, blocks, specs, [out] * XS, scratch, 4)


def combine_kernel(place_ref, want_ref, *refs):
    pieces, outs, totals, largest = refs[: 2 * XS], refs[2 * XS : 3 * XS], refs[3 * XS : -1], refs[-1]
    core = place_ref[2]
    tiles, rows, half = totals[0].shape
    per_owner = tiles // ZS
    chunks = half // LANES
    for total in totals:
        total[...] = jnp.zeros_like(total)
    for side in range(CORES):
        for far in range(XS):
            piece = pieces[side * XS + far]
            row = far * CORES + side
            scales = scale_blocks(piece, XS * ZS * chunks)
            for z in range(ZS):
                for near, total in enumerate(totals):
                    slot = (near + core * (far - near)) * ZS
                    tile = z * per_owner + want_ref[row, slot + z]
                    for chunk in range(chunks):
                        at = (near * ZS + z) * chunks + chunk
                        lanes = slice(chunk * LANES, (chunk + 1) * LANES)
                        total[tile, :, lanes] += numbers(piece[at]) * scales[at]
    for near, total in enumerate(totals):

        def block_of(at):
            return total[at // chunks, :, at % chunks * LANES : (at % chunks + 1) * LANES]

        encode(block_of, tiles * chunks, outs[near], largest.at[near])


def regroup_kernel(*refs):
    pieces, out, largest = refs[:XS], refs[XS], refs[XS + 1]
    rows = out.shape[2]
    count = out.shape[1] - largest.shape[1] // rows
    scales = [scale_blocks(piece, ZS * count) for piece in pieces]
    for z in range(ZS):
        sums = []
        for at in range(z * count, (z + 1) * count):
            sums.append(sum(numbers(piece[at]) * scale[at] for piece, scale in zip(pieces, scales)))
        encode(lambda at: sums[at], count, out, largest.at[z], (z,))


def finish_kernel(place_ref, pieces, keep, send):
    per_owner, rows, half = keep.shape
    chunks = half // LANES
    mine = pl.multiple_of(place_ref[2] * rows, rows)
    scales = [scale_blocks(pieces, per_owner * chunks, (z,)) for z in range(ZS)]
    for out, row in ((keep, mine), (send, rows - mine)):
        row = pl.multiple_of(row, rows)
        for which in range(per_owner):
            for chunk in range(chunks):
                at = which * chunks + chunk
                found = sum(numbers(pieces[z, at, pl.ds(row, rows)]) * scales[z][at] for z in range(ZS))
                out[which, :, chunk * LANES : (chunk + 1) * LANES] = found


def local(amplitudes, tasks, integrals):
    rows, per_owner, width = amplitudes.shape
    half = width // 2
    entries = XS * ZS
    part = CORES * rows
    kind = amplitudes.dtype
    place = jnp.stack([lax.axis_index(axis) for axis in PLANE]).astype(jnp.int32)
    x, core = place[0], place[2]

    def in_order(own, other, axis):
        found = jnp.concatenate([own, other], axis=axis)
        return jnp.where(core == 0, found, jnp.concatenate([other, own], axis=axis))

    tiles = amplitudes.transpose(1, 0, 2)
    low, high = tiles[..., :half], tiles[..., half:]
    own, other = jnp.where(core == 0, low, high), jnp.where(core == 0, high, low)
    tiles = in_order(own, trade(other), 1)
    along_z = swap(jnp.broadcast_to(tiles[None], (ZS, *tiles.shape)), "z")
    gathered = [along_z] + [move(along_z, near, True) for near in range(1, XS)]

    names = tasks.reshape(-1)
    owner = names * 171 >> 9
    slots = ((x - (owner // ZS)) & (XS - 1)) * ZS + (owner & (ZS - 1))
    lane = lax.broadcasted_iota(jnp.int32, (names.shape[0], LANES), 1)
    which = (names - owner * per_owner)[:, None]
    want = jnp.max(jnp.where(slots[:, None] == lane, which, 0), axis=0, keepdims=True)
    want = jnp.concatenate([want, trade(want)])
    wants = jnp.concatenate([want] + [move(want, -far, False) for far in range(1, XS)])

    piece = jax.ShapeDtypeStruct((entries, part, half), kind)
    packed = call(pack_kernel, [piece] * (2 * XS), [SMEM] * 2 + [VMEM] * XS)(place, wants, *gathered)
    direct, via = packed[:XS], packed[XS:]
    via = [trade(v) if far == 0 else move(v, far, False, 1) for far, v in enumerate(via)]
    direct = [v if far == 0 else move(v, far, False) for far, v in enumerate(direct)]

    begun = begin(slots, place, direct, integrals)
    codes = end(0, slots, place, via, begun, integrals)
    onward = end(1, slots, place, via, begun, integrals)
    direct = [v if far == 0 else move(v, -far, False) for far, v in enumerate(codes)]
    via = [trade(v) if far == 0 else move(v, -far, True, 1) for far, v in enumerate(onward)]
    tiles = ZS * per_owner
    chunks = half // LANES
    count = tiles * chunks
    cut = jax.ShapeDtypeStruct((count + extra(count, part), part, LANES), jnp.int16)
    by_near = call(
        combine_kernel,
        [cut] * XS,
        [SMEM] * 2 + [VMEM] * (2 * XS),
        [pltpu.VMEM((tiles, part, half), jnp.float32)] * XS
        + [pltpu.VMEM((XS, extra(count, part) * part, LANES), jnp.float32)],
    )(place, wants, *direct, *via)
    by_near = [v if near == 0 else move(v, -near, True) for near, v in enumerate(by_near)]
    count = per_owner * chunks
    cut = jax.ShapeDtypeStruct((ZS, count + extra(count, part), part, LANES), jnp.int16)
    largest = pltpu.VMEM((ZS, extra(count, part) * part, LANES), jnp.float32)
    by_z = swap(call(regroup_kernel, cut, [VMEM] * XS, [largest])(*by_near), "z")
    out = jax.ShapeDtypeStruct((per_owner, rows, half), jnp.float32)
    keep, send = call(finish_kernel, [out] * 2, [SMEM, VMEM])(place, by_z)
    return in_order(keep, trade(send), 2).transpose(1, 0, 2)


def solution(mesh):
    fine = Mesh(mesh.devices.reshape(XS, ZS, YS, CORES), ("x", "z", "y", "core"))
    tile, pair = ("x", "z"), ("y", "core")
    return jax.shard_map(
        local,
        mesh=fine,
        in_specs=(P(pair, tile, None), P(tile + pair, None), P(tile + pair, None, None)),
        out_specs=P(pair, tile, None),
        check_vma=False,
    )
```

profile of v0, /device:TPU:1, one launch (start us, length us, event | category | flops | bytes accessed | tf_op | source)
XLA Modules:
  0.0 149.2 jit_solution(18423999414977830080)
XLA Ops:
  0.0 0.8 broadcast_select_fusion.1
  0.8 3.2 %collective-permute-start.4 = (bf16[3,16,256]{2,1,0:T(8,128)(2,1)S(1)}, bf16[3,16,256]{2,1,0:T(8,128)(2,1)S(1)}, u32[]{:S(2)}, u32[]{:S(2)}) collective-permute-start(bf16[3,16,256]{2,1,0:T(8,128)(2,1)S(1)} %get-tuple-element.50), channel_id=1, source_target_pairs={{0,1},{1,0},{2,3},{3,2},{4,5},{5,4},{6,7},{7,6},{8,9},{9,8},{10,11... | collective-permute-start | bytes 73736 | tf_op jit(solution)/shard_map/ppermute | solution.py:74
  4.0 0.8 collective-permute-done.4
  4.9 0.8 broadcast_in_dim.26
  5.7 6.4 %all-to-all-start = ((bf16[8,3,32,256]{3,2,1,0:T(8,128)(2,1)}), bf16[8,3,32,256]{3,2,1,0:T(8,128)(2,1)S(1)}, u32[]{:S(2)}, u32[]{:S(2)}) async-start(bf16[8,3,32,256]{3,2,1,0:T(8,128)(2,1)} %broadcast_in_dim.26), calls=%async_computation | async-start | bytes 786432 | tf_op jit(solution)/shard_map/all_to_all | solution.py:27
  12.1 0.8 copy.6
  12.9 0.1 reshape.66
  13.0 14.3 %all-to-all-done.refs_0_ = bf16[8,3,32,256]{3,2,1,0:T(8,128)(2,1)S(1)} async-done(((bf16[8,3,32,256]{3,2,1,0:T(8,128)(2,1)}), bf16[8,3,32,256]{3,2,1,0:T(8,128)(2,1)S(1)}, u32[]{:S(2)}, u32[]{:S(2)}) %all-to-all-start) | async-done | bytes 393248 | tf_op jit(solution)/shard_map/all_to_all | solution.py:27
  27.3 1.3 collective-permute-start.5
  28.6 2.6 %collective-permute-start.6 = (bf16[8,3,32,256]{3,2,1,0:T(8,128)(2,1)S(1)}, bf16[8,3,32,256]{3,2,1,0:T(8,128)(2,1)S(1)}, u32[]{:S(2)}, u32[]{:S(2)}) collective-permute-start(bf16[8,3,32,256]{3,2,1,0:T(8,128)(2,1)S(1)} %all-to-all-done.refs_0_), channel_id=1, source_target_pairs={{0,128},{1,5},{2,130},{3,7},{4,132},{5,1},{6,134},{7,3},{8,136},{9... | collective-permute-start | bytes 1179656 | tf_op jit(solution)/shard_map/ppermute | solution.py:70
  31.2 1.1 collective-permute-start.7
  32.3 0.1 select_reduce_fusion
  32.4 1.2 collective-permute-start
  33.6 0.8 collective-permute-done
  34.4 1.6 %collective-permute-start.1 = (s32[2,128]{1,0:T(2,128)S(1)}, s32[2,128]{1,0:T(2,128)S(1)}, u32[]{:S(2)}, u32[]{:S(2)}) collective-permute-start(s32[2,128]{1,0:T(2,128)S(1)} %pad_add_fusion), channel_id=1, source_target_pairs={{0,6},{1,193},{2,0},{3,195},{4,2},{5,197},{6,4},{7,199},{8,14},{9,... | collective-permute-start | bytes 3080 | tf_op jit(solution)/shard_map/ppermute | solution.py:70
  36.1 0.5 collective-permute-start.2
  36.6 0.4 collective-permute-done.1
  36.9 2.6 %collective-permute-start.3 = (s32[2,128]{1,0:T(2,128)S(1)}, s32[2,128]{1,0:T(2,128)S(1)}, u32[]{:S(2)}, u32[]{:S(2)}) collective-permute-start(s32[2,128]{1,0:T(2,128)S(1)} %pad_add_fusion), channel_id=1, source_target_pairs={{0,2},{1,65},{2,4},{3,67},{4,6},{5,69},{6,0},{7,71},{8,10},{9,73},... | collective-permute-start | bytes 3080 | tf_op jit(solution)/shard_map/ppermute | solution.py:70
  39.5 0.1 pad_add_fusion.1.place_ref
  39.6 0.8 collective-permute-done.2
  40.4 1.1 collective-permute-done.3
  41.4 0.0 collective-permute-done.5.refs_1_
  41.4 0.0 collective-permute-done.6.refs_2_
  41.5 0.0 collective-permute-done.7.refs_3_
  41.5 1.1 shard_map.37
  42.6 0.9 collective-permute-start.12
  43.5 1.9 %collective-permute-start.13 = (bf16[32,32,256]{2,1,0:T(8,128)(2,1)S(1)}, bf16[32,32,256]{2,1,0:T(8,128)(2,1)S(1)}, u32[]{:S(2)}, u32[]{:S(2)}) collective-permute-start(bf16[32,32,256]{2,1,0:T(8,128)(2,1)S(1)} %get-tuple-element.33), channel_id=1, source_target_pairs={{0,4},{1,129},{2,6},{3,131},{4,0},{5,133},{6,2},{7,135},{8,12},{9,... | collective-permute-start | bytes 1572872 | tf_op jit(solution)/shard_map/ppermute | solution.py:70
  45.4 1.2 collective-permute-start.14
  46.6 5.0 %collective-permute-start.10 = (bf16[32,32,256]{2,1,0:T(8,128)(2,1)S(1)}, bf16[32,32,256]{2,1,0:T(8,128)(2,1)S(1)}, u32[]{:S(2)}, u32[]{:S(2)}) collective-permute-start(bf16[32,32,256]{2,1,0:T(8,128)(2,1)S(1)} %get-tuple-element.29), channel_id=1, source_target_pairs={{0,5},{1,128},{2,7},{3,130},{4,1},{5,132},{6,3},{7,134},{8,13},{9,... | collective-permute-start | bytes 1572872 | tf_op jit(solution)/shard_map/ppermute | solution.py:70
  51.5 0.0 collective-permute-start.11
  51.5 0.7 collective-permute-done.12.refs_1_
  52.2 3.6 %collective-permute-start.8 = (bf16[32,32,256]{2,1,0:T(8,128)(2,1)S(1)}, bf16[32,32,256]{2,1,0:T(8,128)(2,1)S(1)}, u32[]{:S(2)}, u32[]{:S(2)}) collective-permute-start(bf16[32,32,256]{2,1,0:T(8,128)(2,1)S(1)} %get-tuple-element.27), channel_id=1, source_target_pairs={{0,1},{1,0},{2,3},{3,2},{4,5},{5,4},{6,7},{7,6},{8,9},{9,8},{10,11... | collective-permute-start | bytes 1572872 | tf_op jit(solution)/shard_map/ppermute | solution.py:74
  55.8 2.1 %collective-permute-done.13.refs_2_ = bf16[32,32,256]{2,1,0:T(8,128)(2,1)S(1)} collective-permute-done((bf16[32,32,256]{2,1,0:T(8,128)(2,1)S(1)}, bf16[32,32,256]{2,1,0:T(8,128)(2,1)S(1)}, u32[]{:S(2)}, u32[]{:S(2)}) %collective-permute-start.13) | collective-permute-done | bytes 524320 | tf_op jit(solution)/shard_map/ppermute | solution.py:70
  57.9 4.1 %collective-permute-start.9 = (bf16[32,32,256]{2,1,0:T(8,128)(2,1)S(1)}, bf16[32,32,256]{2,1,0:T(8,128)(2,1)S(1)}, u32[]{:S(2)}, u32[]{:S(2)}) collective-permute-start(bf16[32,32,256]{2,1,0:T(8,128)(2,1)S(1)} %get-tuple-element.28), channel_id=1, source_target_pairs={{0,3},{1,64},{2,5},{3,66},{4,7},{5,68},{6,1},{7,70},{8,11},{9,72},... | collective-permute-start | bytes 1572872 | tf_op jit(solution)/shard_map/ppermute | solution.py:70
  62.0 0.0 collective-permute-done.14.refs_3_
  62.0 8.3 %shard_map.38.refs_4_ = f32[2,32,128,256]{3,2,1,0:T(8,128)S(1)} custom-call(s32[48]{0:T(128)S(1)} %get-tuple-element.51.slot_ref, s32[3]{0:T(128)S(1)} %pad_add_fusion.1.place_ref, bf16[32,32,256]{2,1,0:T(8,128)(2,1)S(1)} %get-tuple-element.31.refs_0_, bf16[32,32,256]{2,1,0:T(8,128)(2,1)S(1)} %collective-permute-done.12.refs_1_, ...), custom_call_target="tpu_custom_call" | custom-call | flops 1610612736 | bytes 12582912 | tf_op jit(solution)/shard_map/pallas_call | solution.py:189
  70.3 2.6 %collective-permute-done.11.refs_3_ = bf16[32,32,256]{2,1,0:T(8,128)(2,1)S(1)} collective-permute-done((bf16[32,32,256]{2,1,0:T(8,128)(2,1)S(1)}, bf16[32,32,256]{2,1,0:T(8,128)(2,1)S(1)}, u32[]{:S(2)}, u32[]{:S(2)}) %collective-permute-start.11) | collective-permute-done | bytes 524320 | tf_op jit(solution)/shard_map/ppermute | solution.py:70
  72.9 0.0 collective-permute-done.9.refs_1_
  72.9 6.2 %shard_map.40 = (s16[66,32,128]{2,1,0:T(8,128)(2,1)S(1)}, s16[66,32,128]{2,1,0:T(8,128)(2,1)S(1)}, s16[66,32,128]{2,1,0:T(8,128)(2,1)S(1)}, s16[66,32,128]{2,1,0:T(8,128)(2,1)S(1)}) custom-call(s32[48]{0:T(128)S(1)} %get-tuple-element.51.slot_ref, s32[3]{0:T(128)S(1)} %pad_add_fusion.1.place_ref, bf16[32,32,256]{2,1,0:T(8,128)(2,1)S(1)} %collective-permute-done.8.refs_0_, ...), custom_call_target="tpu_custom_call" | custom-call | flops 805306368 | bytes 6291456 | tf_op jit(solution)/shard_map/pallas_call | solution.py:189
  79.2 0.1 collective-permute-start.18
  79.3 3.0 %collective-permute-start.19 = (s16[66,32,128]{2,1,0:T(8,128)(2,1)S(1)}, s16[66,32,128]{2,1,0:T(8,128)(2,1)S(1)}, u32[]{:S(2)}, u32[]{:S(2)}) collective-permute-start(s16[66,32,128]{2,1,0:T(8,128)(2,1)S(1)} %get-tuple-element.40), channel_id=1, source_target_pairs={{0,193},{1,6},{2,195},{3,0},{4,197},{5,2},{6,199},{7,4},{8,201},{9... | collective-permute-start | bytes 1622024 | tf_op jit(solution)/shard_map/ppermute | solution.py:70
  82.3 1.8 %collective-permute-start.20 = (s16[66,32,128]{2,1,0:T(8,128)(2,1)S(1)}, s16[66,32,128]{2,1,0:T(8,128)(2,1)S(1)}, u32[]{:S(2)}, u32[]{:S(2)}) collective-permute-start(s16[66,32,128]{2,1,0:T(8,128)(2,1)S(1)} %get-tuple-element.41), channel_id=1, source_target_pairs={{0,129},{1,4},{2,131},{3,6},{4,133},{5,0},{6,135},{7,2},{8,137},{9... | collective-permute-start | bytes 1622024 | tf_op jit(solution)/shard_map/ppermute | solution.py:70
  84.1 0.1 collective-permute-start.21
  84.2 6.2 %shard_map.39 = (s16[66,32,128]{2,1,0:T(8,128)(2,1)S(1)}, s16[66,32,128]{2,1,0:T(8,128)(2,1)S(1)}, s16[66,32,128]{2,1,0:T(8,128)(2,1)S(1)}, s16[66,32,128]{2,1,0:T(8,128)(2,1)S(1)}) custom-call(s32[48]{0:T(128)S(1)} %get-tuple-element.51.slot_ref, s32[3]{0:T(128)S(1)} %pad_add_fusion.1.place_ref, bf16[32,32,256]{2,1,0:T(8,128)(2,1)S(1)} %collective-permute-done.8.refs_0_, ...), custom_call_target="tpu_custom_call" | custom-call | flops 805306368 | bytes 6291456 | tf_op jit(solution)/shard_map/pallas_call | solution.py:189
  90.4 1.4 collective-permute-start.15
  91.9 0.8 collective-permute-start.16
  92.6 3.1 %collective-permute-done.19.refs_5_ = s16[66,32,128]{2,1,0:T(8,128)(2,1)S(1)} collective-permute-done((s16[66,32,128]{2,1,0:T(8,128)(2,1)S(1)}, s16[66,32,128]{2,1,0:T(8,128)(2,1)S(1)}, u32[]{:S(2)}, u32[]{:S(2)}) %collective-permute-start.19) | collective-permute-done | bytes 540704 | tf_op jit(solution)/shard_map/ppermute | solution.py:70
  95.7 0.0 collective-permute-start.17
  95.7 0.0 collective-permute-done.20.refs_6_
  95.7 9.5 %collective-permute-done.21.refs_7_ = s16[66,32,128]{2,1,0:T(8,128)(2,1)S(1)} collective-permute-done((s16[66,32,128]{2,1,0:T(8,128)(2,1)S(1)}, s16[66,32,128]{2,1,0:T(8,128)(2,1)S(1)}, u32[]{:S(2)}, u32[]{:S(2)}) %collective-permute-start.21) | collective-permute-done | bytes 540704 | tf_op jit(solution)/shard_map/ppermute | solution.py:70
  105.2 4.8 %collective-permute-done.17.refs_3_ = s16[66,32,128]{2,1,0:T(8,128)(2,1)S(1)} collective-permute-done((s16[66,32,128]{2,1,0:T(8,128)(2,1)S(1)}, s16[66,32,128]{2,1,0:T(8,128)(2,1)S(1)}, u32[]{:S(2)}, u32[]{:S(2)}) %collective-permute-start.17) | collective-permute-done | bytes 540704 | tf_op jit(solution)/shard_map/ppermute | solution.py:70
  110.0 2.9 %shard_map.41 = (s16[50,32,128]{2,1,0:T(8,128)(2,1)S(1)}, s16[50,32,128]{2,1,0:T(8,128)(2,1)S(1)}, s16[50,32,128]{2,1,0:T(8,128)(2,1)S(1)}, s16[50,32,128]{2,1,0:T(8,128)(2,1)S(1)}) custom-call(s32[3]{0:T(128)S(1)} %pad_add_fusion.1.place_ref, s32[8,128]{1,0:T(8,128)S(1)} %concatenate.28.want_ref, s16[66,32,128]{2,1,0:T(8,128)(2,1)S(1)} %get-tuple-element.35.refs_0_, ...), custom_call_target="tpu_custom_call" | custom-call | tf_op jit(solution)/shard_map/pallas_call | solution.py:337
  112.9 1.1 collective-permute-start.22
  114.0 0.2 collective-permute-start.23
  114.1 0.5 collective-permute-start.24
  114.7 5.1 %collective-permute-done.22.refs_1_ = s16[50,32,128]{2,1,0:T(8,128)(2,1)S(1)} collective-permute-done((s16[50,32,128]{2,1,0:T(8,128)(2,1)S(1)}, s16[50,32,128]{2,1,0:T(8,128)(2,1)S(1)}, u32[]{:S(2)}, u32[]{:S(2)}) %collective-permute-start.22) | collective-permute-done | bytes 409632 | tf_op jit(solution)/shard_map/ppermute | solution.py:70
  119.7 2.9 %collective-permute-done.23.refs_2_ = s16[50,32,128]{2,1,0:T(8,128)(2,1)S(1)} collective-permute-done((s16[50,32,128]{2,1,0:T(8,128)(2,1)S(1)}, s16[50,32,128]{2,1,0:T(8,128)(2,1)S(1)}, u32[]{:S(2)}, u32[]{:S(2)}) %collective-permute-start.23) | collective-permute-done | bytes 409632 | tf_op jit(solution)/shard_map/ppermute | solution.py:70
  122.6 4.2 %collective-permute-done.24.refs_3_ = s16[50,32,128]{2,1,0:T(8,128)(2,1)S(1)} collective-permute-done((s16[50,32,128]{2,1,0:T(8,128)(2,1)S(1)}, s16[50,32,128]{2,1,0:T(8,128)(2,1)S(1)}, u32[]{:S(2)}, u32[]{:S(2)}) %collective-permute-start.24) | collective-permute-done | bytes 409632 | tf_op jit(solution)/shard_map/ppermute | solution.py:70
  126.8 0.7 shard_map.42
  127.5 15.0 %all_to_all.10.pieces = s16[8,7,32,128]{3,2,1,0:T(8,128)(2,1)S(1)} all-to-all(s16[8,7,32,128]{3,2,1,0:T(8,128)(2,1)S(1)} %shard_map.42), channel_id=1, replica_groups=mesh['x'=4,'z'=8,'y'=4,'core'=2] {'z'}, dimensions={0} | all-to-all | bytes 917504 | tf_op jit(solution)/shard_map/all_to_all | solution.py:27
  142.5 0.7 shard_map.43
  143.2 4.5 %collective-permute-start.25 = (f32[3,16,256]{2,1,0:T(8,128)S(1)}, f32[3,16,256]{2,1,0:T(8,128)S(1)}, u32[]{:S(2)}, u32[]{:S(2)}) collective-permute-start(f32[3,16,256]{2,1,0:T(8,128)S(1)} %get-tuple-element.48), channel_id=1, source_target_pairs={{0,1},{1,0},{2,3},{3,2},{4,5},{5,4},{6,7},{7,6},{8,9},{9,8},{10,11... | collective-permute-start | bytes 147464 | tf_op jit(solution)/shard_map/ppermute | solution.py:74
  147.7 0.9 collective-permute-done.25
  148.6 0.6 fusion
  (9 shorter events, 0.1 us)
Async XLA Ops:
  0.8 4.1 %collective-permute-start.4 = (bf16[3,16,256]{2,1,0:T(8,128)(2,1)S(1)}, bf16[3,16,256]{2,1,0:T(8,128)(2,1)S(1)}, u32[]{:S(2)}, u32[]{:S(2)}) collective-permute-start(bf16[3,16,256]{2,1,0:T(8,128)(2,1)S(1)} %get-tuple-element.50), channel_id=1, source_target_pairs={{0,1},{1,0},{2,3},{3,2},{4,5},{5,4},{6,7},{7,6},{8,9},{9,8},{10,11... | collective-permute-start | bytes 73736 | tf_op jit(solution)/shard_map/ppermute | solution.py:74
  5.7 21.6 %all-to-all-start = ((bf16[8,3,32,256]{3,2,1,0:T(8,128)(2,1)}), bf16[8,3,32,256]{3,2,1,0:T(8,128)(2,1)S(1)}, u32[]{:S(2)}, u32[]{:S(2)}) async-start(bf16[8,3,32,256]{3,2,1,0:T(8,128)(2,1)} %broadcast_in_dim.26), calls=%async_computation | async-start | bytes 786432 | tf_op jit(solution)/shard_map/all_to_all | solution.py:27
  27.3 14.2 %collective-permute-start.5 = (bf16[8,3,32,256]{3,2,1,0:T(8,128)(2,1)S(1)}, bf16[8,3,32,256]{3,2,1,0:T(8,128)(2,1)S(1)}, u32[]{:S(2)}, u32[]{:S(2)}) collective-permute-start(bf16[8,3,32,256]{3,2,1,0:T(8,128)(2,1)S(1)} %all-to-all-done.refs_0_), channel_id=1, source_target_pairs={{0,64},{1,3},{2,66},{3,5},{4,68},{5,7},{6,70},{7,1},{8,72},{9,11},... | collective-permute-start | bytes 1179656 | tf_op jit(solution)/shard_map/ppermute | solution.py:70
  28.6 12.9 %collective-permute-start.6 = (bf16[8,3,32,256]{3,2,1,0:T(8,128)(2,1)S(1)}, bf16[8,3,32,256]{3,2,1,0:T(8,128)(2,1)S(1)}, u32[]{:S(2)}, u32[]{:S(2)}) collective-permute-start(bf16[8,3,32,256]{3,2,1,0:T(8,128)(2,1)S(1)} %all-to-all-done.refs_0_), channel_id=1, source_target_pairs={{0,128},{1,5},{2,130},{3,7},{4,132},{5,1},{6,134},{7,3},{8,136},{9... | collective-permute-start | bytes 1179656 | tf_op jit(solution)/shard_map/ppermute | solution.py:70
  31.2 10.3 %collective-permute-start.7 = (bf16[8,3,32,256]{3,2,1,0:T(8,128)(2,1)S(1)}, bf16[8,3,32,256]{3,2,1,0:T(8,128)(2,1)S(1)}, u32[]{:S(2)}, u32[]{:S(2)}) collective-permute-start(bf16[8,3,32,256]{3,2,1,0:T(8,128)(2,1)S(1)} %all-to-all-done.refs_0_), channel_id=1, source_target_pairs={{0,192},{1,7},{2,194},{3,1},{4,196},{5,3},{6,198},{7,5},{8,200},{9... | collective-permute-start | bytes 1179656 | tf_op jit(solution)/shard_map/ppermute | solution.py:70
  32.4 2.1 %collective-permute-start = (s32[1,128]{1,0:T(1,128)S(1)}, s32[1,128]{1,0:T(1,128)S(1)}, u32[]{:S(2)}, u32[]{:S(2)}) collective-permute-start(s32[1,128]{1,0:T(1,128)S(1)} %bitcast.8), channel_id=1, source_target_pairs={{0,1},{1,0},{2,3},{3,2},{4,5},{5,4},{6,7},{7,6},{8,9},{9,8},{10,11... | collective-permute-start | bytes 1544 | tf_op jit(solution)/shard_map/ppermute | solution.py:74
  34.4 2.5 %collective-permute-start.1 = (s32[2,128]{1,0:T(2,128)S(1)}, s32[2,128]{1,0:T(2,128)S(1)}, u32[]{:S(2)}, u32[]{:S(2)}) collective-permute-start(s32[2,128]{1,0:T(2,128)S(1)} %pad_add_fusion), channel_id=1, source_target_pairs={{0,6},{1,193},{2,0},{3,195},{4,2},{5,197},{6,4},{7,199},{8,14},{9,... | collective-permute-start | bytes 3080 | tf_op jit(solution)/shard_map/ppermute | solution.py:70
  36.1 4.3 %collective-permute-start.2 = (s32[2,128]{1,0:T(2,128)S(1)}, s32[2,128]{1,0:T(2,128)S(1)}, u32[]{:S(2)}, u32[]{:S(2)}) collective-permute-start(s32[2,128]{1,0:T(2,128)S(1)} %pad_add_fusion), channel_id=1, source_target_pairs={{0,4},{1,129},{2,6},{3,131},{4,0},{5,133},{6,2},{7,135},{8,12},{9,... | collective-permute-start | bytes 3080 | tf_op jit(solution)/shard_map/ppermute | solution.py:70
  36.9 4.5 %collective-permute-start.3 = (s32[2,128]{1,0:T(2,128)S(1)}, s32[2,128]{1,0:T(2,128)S(1)}, u32[]{:S(2)}, u32[]{:S(2)}) collective-permute-start(s32[2,128]{1,0:T(2,128)S(1)} %pad_add_fusion), channel_id=1, source_target_pairs={{0,2},{1,65},{2,4},{3,67},{4,6},{5,69},{6,0},{7,71},{8,10},{9,73},... | collective-permute-start | bytes 3080 | tf_op jit(solution)/shard_map/ppermute | solution.py:70
  42.6 9.6 %collective-permute-start.12 = (bf16[32,32,256]{2,1,0:T(8,128)(2,1)S(1)}, bf16[32,32,256]{2,1,0:T(8,128)(2,1)S(1)}, u32[]{:S(2)}, u32[]{:S(2)}) collective-permute-start(bf16[32,32,256]{2,1,0:T(8,128)(2,1)S(1)} %get-tuple-element.32), channel_id=1, source_target_pairs={{0,2},{1,65},{2,4},{3,67},{4,6},{5,69},{6,0},{7,71},{8,10},{9,73},... | collective-permute-start | bytes 1572872 | tf_op jit(solution)/shard_map/ppermute | solution.py:70
  43.5 14.4 %collective-permute-start.13 = (bf16[32,32,256]{2,1,0:T(8,128)(2,1)S(1)}, bf16[32,32,256]{2,1,0:T(8,128)(2,1)S(1)}, u32[]{:S(2)}, u32[]{:S(2)}) collective-permute-start(bf16[32,32,256]{2,1,0:T(8,128)(2,1)S(1)} %get-tuple-element.33), channel_id=1, source_target_pairs={{0,4},{1,129},{2,6},{3,131},{4,0},{5,133},{6,2},{7,135},{8,12},{9,... | collective-permute-start | bytes 1572872 | tf_op jit(solution)/shard_map/ppermute | solution.py:70
  45.4 16.6 %collective-permute-start.14 = (bf16[32,32,256]{2,1,0:T(8,128)(2,1)S(1)}, bf16[32,32,256]{2,1,0:T(8,128)(2,1)S(1)}, u32[]{:S(2)}, u32[]{:S(2)}) collective-permute-start(bf16[32,32,256]{2,1,0:T(8,128)(2,1)S(1)} %get-tuple-element.34), channel_id=1, source_target_pairs={{0,6},{1,193},{2,0},{3,195},{4,2},{5,197},{6,4},{7,199},{8,14},{9,... | collective-permute-start | bytes 1572872 | tf_op jit(solution)/shard_map/ppermute | solution.py:70
  46.6 23.7 %collective-permute-start.10 = (bf16[32,32,256]{2,1,0:T(8,128)(2,1)S(1)}, bf16[32,32,256]{2,1,0:T(8,128)(2,1)S(1)}, u32[]{:S(2)}, u32[]{:S(2)}) collective-permute-start(bf16[32,32,256]{2,1,0:T(8,128)(2,1)S(1)} %get-tuple-element.29), channel_id=1, source_target_pairs={{0,5},{1,128},{2,7},{3,130},{4,1},{5,132},{6,3},{7,134},{8,13},{9,... | collective-permute-start | bytes 1572872 | tf_op jit(solution)/shard_map/ppermute | solution.py:70
  51.5 21.4 %collective-permute-start.11 = (bf16[32,32,256]{2,1,0:T(8,128)(2,1)S(1)}, bf16[32,32,256]{2,1,0:T(8,128)(2,1)S(1)}, u32[]{:S(2)}, u32[]{:S(2)}) collective-permute-start(bf16[32,32,256]{2,1,0:T(8,128)(2,1)S(1)} %get-tuple-element.30), channel_id=1, source_target_pairs={{0,7},{1,192},{2,1},{3,194},{4,3},{5,196},{6,5},{7,198},{8,15},{9,... | collective-permute-start | bytes 1572872 | tf_op jit(solution)/shard_map/ppermute | solution.py:70
  52.2 20.7 %collective-permute-start.8 = (bf16[32,32,256]{2,1,0:T(8,128)(2,1)S(1)}, bf16[32,32,256]{2,1,0:T(8,128)(2,1)S(1)}, u32[]{:S(2)}, u32[]{:S(2)}) collective-permute-start(bf16[32,32,256]{2,1,0:T(8,128)(2,1)S(1)} %get-tuple-element.27), channel_id=1, source_target_pairs={{0,1},{1,0},{2,3},{3,2},{4,5},{5,4},{6,7},{7,6},{8,9},{9,8},{10,11... | collective-permute-start | bytes 1572872 | tf_op jit(solution)/shard_map/ppermute | solution.py:74
  57.9 15.0 %collective-permute-start.9 = (bf16[32,32,256]{2,1,0:T(8,128)(2,1)S(1)}, bf16[32,32,256]{2,1,0:T(8,128)(2,1)S(1)}, u32[]{:S(2)}, u32[]{:S(2)}) collective-permute-start(bf16[32,32,256]{2,1,0:T(8,128)(2,1)S(1)} %get-tuple-element.28), channel_id=1, source_target_pairs={{0,3},{1,64},{2,5},{3,66},{4,7},{5,68},{6,1},{7,70},{8,11},{9,72},... | collective-permute-start | bytes 1572872 | tf_op jit(solution)/shard_map/ppermute | solution.py:70
  79.2 12.7 %collective-permute-start.18 = (s16[66,32,128]{2,1,0:T(8,128)(2,1)S(1)}, s16[66,32,128]{2,1,0:T(8,128)(2,1)S(1)}, u32[]{:S(2)}, u32[]{:S(2)}) collective-permute-start(s16[66,32,128]{2,1,0:T(8,128)(2,1)S(1)} %get-tuple-element.39), channel_id=1, source_target_pairs={{0,1},{1,0},{2,3},{3,2},{4,5},{5,4},{6,7},{7,6},{8,9},{9,8},{10,11... | collective-permute-start | bytes 1622024 | tf_op jit(solution)/shard_map/ppermute | solution.py:74
  79.3 16.4 %collective-permute-start.19 = (s16[66,32,128]{2,1,0:T(8,128)(2,1)S(1)}, s16[66,32,128]{2,1,0:T(8,128)(2,1)S(1)}, u32[]{:S(2)}, u32[]{:S(2)}) collective-permute-start(s16[66,32,128]{2,1,0:T(8,128)(2,1)S(1)} %get-tuple-element.40), channel_id=1, source_target_pairs={{0,193},{1,6},{2,195},{3,0},{4,197},{5,2},{6,199},{7,4},{8,201},{9... | collective-permute-start | bytes 1622024 | tf_op jit(solution)/shard_map/ppermute | solution.py:70
  82.3 13.4 %collective-permute-start.20 = (s16[66,32,128]{2,1,0:T(8,128)(2,1)S(1)}, s16[66,32,128]{2,1,0:T(8,128)(2,1)S(1)}, u32[]{:S(2)}, u32[]{:S(2)}) collective-permute-start(s16[66,32,128]{2,1,0:T(8,128)(2,1)S(1)} %get-tuple-element.41), channel_id=1, source_target_pairs={{0,129},{1,4},{2,131},{3,6},{4,133},{5,0},{6,135},{7,2},{8,137},{9... | collective-permute-start | bytes 1622024 | tf_op jit(solution)/shard_map/ppermute | solution.py:70
  84.1 21.1 %collective-permute-start.21 = (s16[66,32,128]{2,1,0:T(8,128)(2,1)S(1)}, s16[66,32,128]{2,1,0:T(8,128)(2,1)S(1)}, u32[]{:S(2)}, u32[]{:S(2)}) collective-permute-start(s16[66,32,128]{2,1,0:T(8,128)(2,1)S(1)} %get-tuple-element.42), channel_id=1, source_target_pairs={{0,65},{1,2},{2,67},{3,4},{4,69},{5,6},{6,71},{7,0},{8,73},{9,10},... | collective-permute-start | bytes 1622024 | tf_op jit(solution)/shard_map/ppermute | solution.py:70
  90.4 14.8 %collective-permute-start.15 = (s16[66,32,128]{2,1,0:T(8,128)(2,1)S(1)}, s16[66,32,128]{2,1,0:T(8,128)(2,1)S(1)}, u32[]{:S(2)}, u32[]{:S(2)}) collective-permute-start(s16[66,32,128]{2,1,0:T(8,128)(2,1)S(1)} %get-tuple-element.36), channel_id=1, source_target_pairs={{0,6},{1,193},{2,0},{3,195},{4,2},{5,197},{6,4},{7,199},{8,14},{9,... | collective-permute-start | bytes 1622024 | tf_op jit(solution)/shard_map/ppermute | solution.py:70
  91.9 13.4 %collective-permute-start.16 = (s16[66,32,128]{2,1,0:T(8,128)(2,1)S(1)}, s16[66,32,128]{2,1,0:T(8,128)(2,1)S(1)}, u32[]{:S(2)}, u32[]{:S(2)}) collective-permute-start(s16[66,32,128]{2,1,0:T(8,128)(2,1)S(1)} %get-tuple-element.37), channel_id=1, source_target_pairs={{0,4},{1,129},{2,6},{3,131},{4,0},{5,133},{6,2},{7,135},{8,12},{9,... | collective-permute-start | bytes 1622024 | tf_op jit(solution)/shard_map/ppermute | solution.py:70
  95.7 14.3 %collective-permute-start.17 = (s16[66,32,128]{2,1,0:T(8,128)(2,1)S(1)}, s16[66,32,128]{2,1,0:T(8,128)(2,1)S(1)}, u32[]{:S(2)}, u32[]{:S(2)}) collective-permute-start(s16[66,32,128]{2,1,0:T(8,128)(2,1)S(1)} %get-tuple-element.38), channel_id=1, source_target_pairs={{0,2},{1,65},{2,4},{3,67},{4,6},{5,69},{6,0},{7,71},{8,10},{9,73},... | collective-permute-start | bytes 1622024 | tf_op jit(solution)/shard_map/ppermute | solution.py:70
  112.9 6.9 %collective-permute-start.22 = (s16[50,32,128]{2,1,0:T(8,128)(2,1)S(1)}, s16[50,32,128]{2,1,0:T(8,128)(2,1)S(1)}, u32[]{:S(2)}, u32[]{:S(2)}) collective-permute-start(s16[50,32,128]{2,1,0:T(8,128)(2,1)S(1)} %get-tuple-element.44), channel_id=1, source_target_pairs={{0,192},{1,7},{2,194},{3,1},{4,196},{5,3},{6,198},{7,5},{8,200},{9... | collective-permute-start | bytes 1228808 | tf_op jit(solution)/shard_map/ppermute | solution.py:70
  114.0 8.6 %collective-permute-start.23 = (s16[50,32,128]{2,1,0:T(8,128)(2,1)S(1)}, s16[50,32,128]{2,1,0:T(8,128)(2,1)S(1)}, u32[]{:S(2)}, u32[]{:S(2)}) collective-permute-start(s16[50,32,128]{2,1,0:T(8,128)(2,1)S(1)} %get-tuple-element.45), channel_id=1, source_target_pairs={{0,128},{1,5},{2,130},{3,7},{4,132},{5,1},{6,134},{7,3},{8,136},{9... | collective-permute-start | bytes 1228808 | tf_op jit(solution)/shard_map/ppermute | solution.py:70
  114.1 12.7 %collective-permute-start.24 = (s16[50,32,128]{2,1,0:T(8,128)(2,1)S(1)}, s16[50,32,128]{2,1,0:T(8,128)(2,1)S(1)}, u32[]{:S(2)}, u32[]{:S(2)}) collective-permute-start(s16[50,32,128]{2,1,0:T(8,128)(2,1)S(1)} %get-tuple-element.46), channel_id=1, source_target_pairs={{0,64},{1,3},{2,66},{3,5},{4,68},{5,7},{6,70},{7,1},{8,72},{9,11},... | collective-permute-start | bytes 1228808 | tf_op jit(solution)/shard_map/ppermute | solution.py:70
  143.2 5.4 %collective-permute-start.25 = (f32[3,16,256]{2,1,0:T(8,128)S(1)}, f32[3,16,256]{2,1,0:T(8,128)S(1)}, u32[]{:S(2)}, u32[]{:S(2)}) collective-permute-start(f32[3,16,256]{2,1,0:T(8,128)S(1)} %get-tuple-element.48), channel_id=1, source_target_pairs={{0,1},{1,0},{2,3},{3,2},{4,5},{5,4},{6,7},{7,6},{8,9},{9,8},{10,11... | collective-permute-start | bytes 147464 | tf_op jit(solution)/shard_map/ppermute | solution.py:74
where the time goes:
time: 150 us; the launch traced here: 149 us
  waiting for transfers between devices  54 us (36%)
  starting transfers between devices  50.8 us (34%)
  Pallas kernels  26.1 us (17%)
  blocking collectives  15 us (10%)
  local copies, waits for them, and re-layouts  1.67 us (1%)
  other arithmetic  1.62 us (1%)
    ppermute x21, waiting for transfers between devices, move(): return lax.ppermute(value, WHOLE, table)  37.1 us
    ppermute x21, starting transfers between devices, move(): return lax.ppermute(value, WHOLE, table)  31.7 us
    pallas_call x3, Pallas kernels, products(): pl.pallas_call(kernel, out_shape=out_shape, grid_spec=pltpu.PrefetchScala...  20.7 us
    all_to_all x1, blocking collectives, swap(): return lax.all_to_all(value, axes, split_axis=0, concat_axis=0, tiled=True)  15 us
    all_to_all x1, waiting for transfers between devices, swap(): return lax.all_to_all(value, axes, split_axis=0, concat_axis=0, tiled=True)  14.3 us
    ppermute x5, starting transfers between devices, trade(): return lax.ppermute(value, 'core', [(0, 1), (1, 0)])  12.7 us
    all_to_all x1, starting transfers between devices, swap(): return lax.all_to_all(value, axes, split_axis=0, concat_axis=0, tiled=True)  6.45 us
  transfers between devices with their start and end apart: 27, of which 16 were waited for; matrix products, arithmetic and copies ran while one was open for 1% of the time, Pallas kernels for 10%

commit v1 on v0

--- a/solution.py
+++ b/solution.py
@@ -11,7 +11,7 @@
 XS, ZS, YS, CORES = 4, 8, 4, 2
 PLANE = ("x", "y", "core")
 WHOLE = ("x", "z", "y", "core")
-PER_STEP = 8
+PER_STEP = 12
 LIMIT = 32
 
 LANES = 128
@@ -108,7 +108,11 @@
             for near in range(XS):
                 slot = (near + core * (far - near)) * ZS
                 for z in range(ZS):
-                    outs[side * XS + far][near * ZS + z] = gathered[near][z, want_ref[row, slot + z]]
+                    which = want_ref[row, slot + z]
+                    for part in range(CORES):
+                        found = gathered[near][z * CORES + part, which]
+                        rows = slice(part * found.shape[0], (part + 1) * found.shape[0])
+                        outs[side * XS + far][near * ZS + z, rows] = found
 
 
 def spot(place_ref, side, far, near, part):
@@ -267,27 +271,29 @@
 def regroup_kernel(*refs):
     pieces, out, largest = refs[:XS], refs[XS], refs[XS + 1]
     rows = out.shape[2]
-    count = out.shape[1] - largest.shape[1] // rows
+    count = out.shape[1] - extra(out.shape[1] - 1, rows)
     scales = [scale_blocks(piece, ZS * count) for piece in pieces]
     for z in range(ZS):
         sums = []
         for at in range(z * count, (z + 1) * count):
             sums.append(sum(numbers(piece[at]) * scale[at] for piece, scale in zip(pieces, scales)))
-        encode(lambda at: sums[at], count, out, largest.at[z], (z,))
-
-
-def finish_kernel(place_ref, pieces, keep, send):
-    per_owner, rows, half = keep.shape
-    chunks = half // LANES
-    mine = pl.multiple_of(place_ref[2] * rows, rows)
-    scales = [scale_blocks(pieces, per_owner * chunks, (z,)) for z in range(ZS)]
-    for out, row in ((keep, mine), (send, rows - mine)):
-        row = pl.multiple_of(row, rows)
+        for core in range(CORES):
+            to = z * CORES + core
+            encode(lambda at: sums[at][core * rows : (core + 1) * rows], count, out, largest.at[to], (to,))
+
+
+def finish_kernel(pieces, out):
+    per_owner, _, width = out.shape
+    chunks = width // CORES // LANES
+    scales = [scale_blocks(pieces, per_owner * chunks, (source,)) for source in range(ZS * CORES)]
+    for core in range(CORES):
         for which in range(per_owner):
             for chunk in range(chunks):
                 at = which * chunks + chunk
-                found = sum(numbers(pieces[z, at, pl.ds(row, rows)]) * scales[z][at] for z in range(ZS))
-                out[which, :, chunk * LANES : (chunk + 1) * LANES] = found
+                sources = [z * CORES + core for z in range(ZS)]
+                found = sum(numbers(pieces[source, at]) * scales[source][at] for source in sources)
+                lane = (core * chunks + chunk) * LANES
+                out[which, :, lane : lane + LANES] = found
 
 
 def local(amplitudes, tasks, integrals):
@@ -297,17 +303,12 @@
     part = CORES * rows
     kind = amplitudes.dtype
     place = jnp.stack([lax.axis_index(axis) for axis in PLANE]).astype(jnp.int32)
-    x, core = place[0], place[2]
-
-    def in_order(own, other, axis):
-        found = jnp.concatenate([own, other], axis=axis)
-        return jnp.where(core == 0, found, jnp.concatenate([other, own], axis=axis))
+    x = place[0]
 
     tiles = amplitudes.transpose(1, 0, 2)
-    low, high = tiles[..., :half], tiles[..., half:]
-    own, other = jnp.where(core == 0, low, high), jnp.where(core == 0, high, low)
-    tiles = in_order(own, trade(other), 1)
-    along_z = swap(jnp.broadcast_to(tiles[None], (ZS, *tiles.shape)), "z")
+    halves = jnp.stack([tiles[..., :half], tiles[..., half:]])
+    halves = jnp.broadcast_to(halves[None], (ZS, *halves.shape)).reshape(-1, *halves.shape[1:])
+    along_z = swap(halves, ("z", "core"))
     gathered = [along_z] + [move(along_z, near, True) for near in range(1, XS)]
 
     names = tasks.reshape(-1)
@@ -343,12 +344,11 @@
     )(place, wants, *direct, *via)
     by_near = [v if near == 0 else move(v, -near, True) for near, v in enumerate(by_near)]
     count = per_owner * chunks
-    cut = jax.ShapeDtypeStruct((ZS, count + extra(count, part), part, LANES), jnp.int16)
-    largest = pltpu.VMEM((ZS, extra(count, part) * part, LANES), jnp.float32)
-    by_z = swap(call(regroup_kernel, cut, [VMEM] * XS, [largest])(*by_near), "z")
-    out = jax.ShapeDtypeStruct((per_owner, rows, half), jnp.float32)
-    keep, send = call(finish_kernel, [out] * 2, [SMEM, VMEM])(place, by_z)
-    return in_order(keep, trade(send), 2).transpose(1, 0, 2)
+    cut = jax.ShapeDtypeStruct((ZS * CORES, count + extra(count, rows), rows, LANES), jnp.int16)
+    largest = pltpu.VMEM((ZS * CORES, extra(count, rows) * rows, LANES), jnp.float32)
+    by_z = swap(call(regroup_kernel, cut, [VMEM] * XS, [largest])(*by_near), ("z", "core"))
+    out = jax.ShapeDtypeStruct((per_owner, rows, width), jnp.float32)
+    return call(finish_kernel, out, [VMEM])(by_z).transpose(1, 0, 2)
 
 
 def solution(mesh):

time: 150 us -> 147 us (0.980)
  waiting for transfers between devices: 54 us -> 49.8 us
  blocking collectives: 15 us -> 17.8 us
  Pallas kernels: 26.1 us -> 24.2 us
    ppermute x5 -> x3, starting transfers between devices: 12.7 us -> 4.72 us  [trade(): return lax.ppermute(value, 'core', [(0, 1), (1, 0)])]
    ppermute x21, starting transfers between devices: 31.7 us -> 36.9 us  [move(): return lax.ppermute(value, WHOLE, table)]
    all_to_all x1, starting transfers between devices: 6.45 us -> 9.98 us  [swap(): return lax.all_to_all(value, axes, split_axis=0, concat_axis=0, tiled=True)]
    all_to_all x1, blocking collectives: 15 us -> 17.8 us  [swap(): return lax.all_to_all(value, axes, split_axis=0, concat_axis=0, tiled=True)]
    ppermute x21, waiting for transfers between devices: 37.1 us -> 35 us  [move(): return lax.ppermute(value, WHOLE, table)]
    pallas_call x3, Pallas kernels: 20.7 us -> 18.7 us  [products(): pl.pallas_call(kernel, out_shape=out_shape, grid_spec=pltpu.PrefetchScala...]
  transfers between devices with their start and end apart: 27 -> 25, of which waited for: 16 -> 13; matrix products, arithmetic and copies ran while one was open for 1% -> 1% of each run, Pallas kernels for 10% -> 9%
where the time goes in v1:
time: 147 us; the launch traced here: 146 us
  starting transfers between devices  51.6 us (35%)
  waiting for transfers between devices  49.8 us (34%)
  Pallas kernels  24.2 us (16%)
  blocking collectives  17.8 us (12%)
  local copies, waits for them, and re-layouts  2.42 us (2%)
    ppermute x21, starting transfers between devices, move(): return lax.ppermute(value, WHOLE, table)  36.9 us
    ppermute x21, waiting for transfers between devices, move(): return lax.ppermute(value, WHOLE, table)  35 us
    pallas_call x3, Pallas kernels, products(): pl.pallas_call(kernel, out_shape=out_shape, grid_spec=pltpu.PrefetchScala...  18.7 us
    all_to_all x1, blocking collectives, swap(): return lax.all_to_all(value, axes, split_axis=0, concat_axis=0, tiled=True)  17.8 us
    all_to_all x1, waiting for transfers between devices, swap(): return lax.all_to_all(value, axes, split_axis=0, concat_axis=0, tiled=True)  13.7 us
    all_to_all x1, starting transfers between devices, swap(): return lax.all_to_all(value, axes, split_axis=0, concat_axis=0, tiled=True)  9.98 us
    ppermute x3, starting transfers between devices, trade(): return lax.ppermute(value, 'core', [(0, 1), (1, 0)])  4.72 us
  transfers between devices with their start and end apart: 25, of which 13 were waited for; matrix products, arithmetic and copies ran while one was open for 1% of the time, Pallas kernels for 9%

profile of v1, /device:TPU:1, one launch (start us, length us, event | category | flops | bytes accessed | tf_op | source)
XLA Modules:
  0.0 146.2 jit_solution(1664225024951954460)
XLA Ops:
  0.0 0.8 slice_bitcast_fusion.1
  0.8 0.8 broadcast_in_dim.26
  1.6 10.0 %all-to-all-start = ((bf16[16,3,16,256]{3,2,1,0:T(8,128)(2,1)}), bf16[16,3,16,256]{3,2,1,0:T(8,128)(2,1)S(1)}, u32[]{:S(2)}, u32[]{:S(2)}) async-start(bf16[16,3,16,256]{3,2,1,0:T(8,128)(2,1)} %bitcast.7), calls=%async_computation | async-start | bytes 786432 | tf_op jit(solution)/shard_map/all_to_all | solution.py:27
  11.5 0.8 copy.6
  12.3 0.1 reshape.41
  12.4 13.7 %all-to-all-done.refs_0_ = bf16[16,3,16,256]{3,2,1,0:T(8,128)(2,1)S(1)} async-done(((bf16[16,3,16,256]{3,2,1,0:T(8,128)(2,1)}), bf16[16,3,16,256]{3,2,1,0:T(8,128)(2,1)S(1)}, u32[]{:S(2)}, u32[]{:S(2)}) %all-to-all-start) | async-done | bytes 393248 | tf_op jit(solution)/shard_map/all_to_all | solution.py:27
  26.1 1.3 collective-permute-start.4
  27.4 2.6 %collective-permute-start.5 = (bf16[16,3,16,256]{3,2,1,0:T(8,128)(2,1)S(1)}, bf16[16,3,16,256]{3,2,1,0:T(8,128)(2,1)S(1)}, u32[]{:S(2)}, u32[]{:S(2)}) collective-permute-start(bf16[16,3,16,256]{3,2,1,0:T(8,128)(2,1)S(1)} %all-to-all-done.refs_0_), channel_id=1, source_target_pairs={{0,128},{1,5},{2,130},{3,7},{4,132},{5,1},{6,134},{7,3},{8,136},{9... | collective-permute-start | bytes 1179656 | tf_op jit(solution)/shard_map/ppermute | solution.py:70
  30.0 1.1 collective-permute-start.6
  31.1 0.1 select_reduce_fusion
  31.2 0.1 collective-permute-start
  31.3 1.1 collective-permute-done
  32.4 2.5 %collective-permute-start.1 = (s32[2,128]{1,0:T(2,128)S(1)}, s32[2,128]{1,0:T(2,128)S(1)}, u32[]{:S(2)}, u32[]{:S(2)}) collective-permute-start(s32[2,128]{1,0:T(2,128)S(1)} %pad_add_fusion), channel_id=1, source_target_pairs={{0,6},{1,193},{2,0},{3,195},{4,2},{5,197},{6,4},{7,199},{8,14},{9,... | collective-permute-start | bytes 3080 | tf_op jit(solution)/shard_map/ppermute | solution.py:70
  34.9 0.5 collective-permute-start.2
  35.4 0.2 collective-permute-done.1
  35.6 1.5 %collective-permute-start.3 = (s32[2,128]{1,0:T(2,128)S(1)}, s32[2,128]{1,0:T(2,128)S(1)}, u32[]{:S(2)}, u32[]{:S(2)}) collective-permute-start(s32[2,128]{1,0:T(2,128)S(1)} %pad_add_fusion), channel_id=1, source_target_pairs={{0,2},{1,65},{2,4},{3,67},{4,6},{5,69},{6,0},{7,71},{8,10},{9,73},... | collective-permute-start | bytes 3080 | tf_op jit(solution)/shard_map/ppermute | solution.py:70
  37.1 0.1 pad_add_fusion.1.place_ref
  37.2 1.9 %collective-permute-done.2 = s32[2,128]{1,0:T(2,128)S(1)} collective-permute-done((s32[2,128]{1,0:T(2,128)S(1)}, s32[2,128]{1,0:T(2,128)S(1)}, u32[]{:S(2)}, u32[]{:S(2)}) %collective-permute-start.2) | collective-permute-done | bytes 1056 | tf_op jit(solution)/shard_map/ppermute | solution.py:70
  39.1 0.9 collective-permute-done.3
  40.0 0.0 collective-permute-done.4.refs_1_
  40.0 0.0 collective-permute-done.5.refs_2_
  40.0 0.0 collective-permute-done.6.refs_3_
  40.1 1.1 shard_map.37
  41.2 0.6 collective-permute-start.11
  41.8 2.5 %collective-permute-start.12 = (bf16[32,32,256]{2,1,0:T(8,128)(2,1)S(1)}, bf16[32,32,256]{2,1,0:T(8,128)(2,1)S(1)}, u32[]{:S(2)}, u32[]{:S(2)}) collective-permute-start(bf16[32,32,256]{2,1,0:T(8,128)(2,1)S(1)} %get-tuple-element.31), channel_id=1, source_target_pairs={{0,4},{1,129},{2,6},{3,131},{4,0},{5,133},{6,2},{7,135},{8,12},{9,... | collective-permute-start | bytes 1572872 | tf_op jit(solution)/shard_map/ppermute | solution.py:70
  44.3 1.2 collective-permute-start.13
  45.4 3.3 %collective-permute-start.10 = (bf16[32,32,256]{2,1,0:T(8,128)(2,1)S(1)}, bf16[32,32,256]{2,1,0:T(8,128)(2,1)S(1)}, u32[]{:S(2)}, u32[]{:S(2)}) collective-permute-start(bf16[32,32,256]{2,1,0:T(8,128)(2,1)S(1)} %get-tuple-element.28), channel_id=1, source_target_pairs={{0,7},{1,192},{2,1},{3,194},{4,3},{5,196},{6,5},{7,198},{8,15},{9,... | collective-permute-start | bytes 1572872 | tf_op jit(solution)/shard_map/ppermute | solution.py:70
  48.7 0.0 collective-permute-start.7
  48.7 2.1 %collective-permute-done.11.refs_1_ = bf16[32,32,256]{2,1,0:T(8,128)(2,1)S(1)} collective-permute-done((bf16[32,32,256]{2,1,0:T(8,128)(2,1)S(1)}, bf16[32,32,256]{2,1,0:T(8,128)(2,1)S(1)}, u32[]{:S(2)}, u32[]{:S(2)}) %collective-permute-start.11) | collective-permute-done | bytes 524320 | tf_op jit(solution)/shard_map/ppermute | solution.py:70
  50.8 3.0 %collective-permute-start.8 = (bf16[32,32,256]{2,1,0:T(8,128)(2,1)S(1)}, bf16[32,32,256]{2,1,0:T(8,128)(2,1)S(1)}, u32[]{:S(2)}, u32[]{:S(2)}) collective-permute-start(bf16[32,32,256]{2,1,0:T(8,128)(2,1)S(1)} %get-tuple-element.26), channel_id=1, source_target_pairs={{0,3},{1,64},{2,5},{3,66},{4,7},{5,68},{6,1},{7,70},{8,11},{9,72},... | collective-permute-start | bytes 1572872 | tf_op jit(solution)/shard_map/ppermute | solution.py:70
  53.8 3.0 %collective-permute-done.12.refs_2_ = bf16[32,32,256]{2,1,0:T(8,128)(2,1)S(1)} collective-permute-done((bf16[32,32,256]{2,1,0:T(8,128)(2,1)S(1)}, bf16[32,32,256]{2,1,0:T(8,128)(2,1)S(1)}, u32[]{:S(2)}, u32[]{:S(2)}) %collective-permute-start.12) | collective-permute-done | bytes 524320 | tf_op jit(solution)/shard_map/ppermute | solution.py:70
  56.7 4.2 %collective-permute-start.9 = (bf16[32,32,256]{2,1,0:T(8,128)(2,1)S(1)}, bf16[32,32,256]{2,1,0:T(8,128)(2,1)S(1)}, u32[]{:S(2)}, u32[]{:S(2)}) collective-permute-start(bf16[32,32,256]{2,1,0:T(8,128)(2,1)S(1)} %get-tuple-element.27), channel_id=1, source_target_pairs={{0,5},{1,128},{2,7},{3,130},{4,1},{5,132},{6,3},{7,134},{8,13},{9,... | collective-permute-start | bytes 1572872 | tf_op jit(solution)/shard_map/ppermute | solution.py:70
  60.9 0.0 collective-permute-done.13.refs_3_
  61.0 7.8 %shard_map.38.refs_4_ = f32[2,32,128,256]{3,2,1,0:T(8,128)S(1)} custom-call(s32[48]{0:T(128)S(1)} %get-tuple-element.47.slot_ref, s32[3]{0:T(128)S(1)} %pad_add_fusion.1.place_ref, bf16[32,32,256]{2,1,0:T(8,128)(2,1)S(1)} %get-tuple-element.29.refs_0_, bf16[32,32,256]{2,1,0:T(8,128)(2,1)S(1)} %collective-permute-done.11.refs_1_, ...), custom_call_target="tpu_custom_call" | custom-call | flops 1610612736 | bytes 12582912 | tf_op jit(solution)/shard_map/pallas_call | solution.py:193
  68.8 0.0 collective-permute-done.10.refs_3_
  68.8 0.0 collective-permute-done.7.refs_0_
  68.8 0.0 collective-permute-done.8.refs_1_
  68.8 1.3 collective-permute-done.9.refs_2_
  70.1 5.5 %shard_map.40 = (s16[66,32,128]{2,1,0:T(8,128)(2,1)S(1)}, s16[66,32,128]{2,1,0:T(8,128)(2,1)S(1)}, s16[66,32,128]{2,1,0:T(8,128)(2,1)S(1)}, s16[66,32,128]{2,1,0:T(8,128)(2,1)S(1)}) custom-call(s32[48]{0:T(128)S(1)} %get-tuple-element.47.slot_ref, s32[3]{0:T(128)S(1)} %pad_add_fusion.1.place_ref, bf16[32,32,256]{2,1,0:T(8,128)(2,1)S(1)} %collective-permute-done.7.refs_0_, ...), custom_call_target="tpu_custom_call" | custom-call | flops 805306368 | bytes 6291456 | tf_op jit(solution)/shard_map/pallas_call | solution.py:193
  75.6 4.6 %collective-permute-start.17 = (s16[66,32,128]{2,1,0:T(8,128)(2,1)S(1)}, s16[66,32,128]{2,1,0:T(8,128)(2,1)S(1)}, u32[]{:S(2)}, u32[]{:S(2)}) collective-permute-start(s16[66,32,128]{2,1,0:T(8,128)(2,1)S(1)} %get-tuple-element.37), channel_id=1, source_target_pairs={{0,1},{1,0},{2,3},{3,2},{4,5},{5,4},{6,7},{7,6},{8,9},{9,8},{10,11... | collective-permute-start | bytes 1622024 | tf_op jit(solution)/shard_map/ppermute | solution.py:74
  80.3 0.0 collective-permute-start.18
  80.3 1.8 %collective-permute-start.19 = (s16[66,32,128]{2,1,0:T(8,128)(2,1)S(1)}, s16[66,32,128]{2,1,0:T(8,128)(2,1)S(1)}, u32[]{:S(2)}, u32[]{:S(2)}) collective-permute-start(s16[66,32,128]{2,1,0:T(8,128)(2,1)S(1)} %get-tuple-element.39), channel_id=1, source_target_pairs={{0,129},{1,4},{2,131},{3,6},{4,133},{5,0},{6,135},{7,2},{8,137},{9... | collective-permute-start | bytes 1622024 | tf_op jit(solution)/shard_map/ppermute | solution.py:70
  82.1 0.4 collective-permute-start.20
  82.5 5.4 %shard_map.39 = (s16[66,32,128]{2,1,0:T(8,128)(2,1)S(1)}, s16[66,32,128]{2,1,0:T(8,128)(2,1)S(1)}, s16[66,32,128]{2,1,0:T(8,128)(2,1)S(1)}, s16[66,32,128]{2,1,0:T(8,128)(2,1)S(1)}) custom-call(s32[48]{0:T(128)S(1)} %get-tuple-element.47.slot_ref, s32[3]{0:T(128)S(1)} %pad_add_fusion.1.place_ref, bf16[32,32,256]{2,1,0:T(8,128)(2,1)S(1)} %collective-permute-done.7.refs_0_, ...), custom_call_target="tpu_custom_call" | custom-call | flops 805306368 | bytes 6291456 | tf_op jit(solution)/shard_map/pallas_call | solution.py:193
  88.0 0.2 collective-permute-start.14
  88.1 0.0 collective-permute-done.17.refs_4_
  88.2 2.4 %collective-permute-start.15 = (s16[66,32,128]{2,1,0:T(8,128)(2,1)S(1)}, s16[66,32,128]{2,1,0:T(8,128)(2,1)S(1)}, u32[]{:S(2)}, u32[]{:S(2)}) collective-permute-start(s16[66,32,128]{2,1,0:T(8,128)(2,1)S(1)} %get-tuple-element.35), channel_id=1, source_target_pairs={{0,4},{1,129},{2,6},{3,131},{4,0},{5,133},{6,2},{7,135},{8,12},{9,... | collective-permute-start | bytes 1622024 | tf_op jit(solution)/shard_map/ppermute | solution.py:70
  90.6 0.0 collective-permute-done.18.refs_5_
  90.6 0.8 collective-permute-start.16
  91.3 0.0 collective-permute-done.19.refs_6_
  91.3 14.2 %collective-permute-done.20.refs_7_ = s16[66,32,128]{2,1,0:T(8,128)(2,1)S(1)} collective-permute-done((s16[66,32,128]{2,1,0:T(8,128)(2,1)S(1)}, s16[66,32,128]{2,1,0:T(8,128)(2,1)S(1)}, u32[]{:S(2)}, u32[]{:S(2)}) %collective-permute-start.20) | collective-permute-done | bytes 540704 | tf_op jit(solution)/shard_map/ppermute | solution.py:70
  105.5 0.0 collective-permute-done.14.refs_1_
  105.5 0.0 collective-permute-done.15.refs_2_
  105.5 2.4 %collective-permute-done.16.refs_3_ = s16[66,32,128]{2,1,0:T(8,128)(2,1)S(1)} collective-permute-done((s16[66,32,128]{2,1,0:T(8,128)(2,1)S(1)}, s16[66,32,128]{2,1,0:T(8,128)(2,1)S(1)}, u32[]{:S(2)}, u32[]{:S(2)}) %collective-permute-start.16) | collective-permute-done | bytes 540704 | tf_op jit(solution)/shard_map/ppermute | solution.py:70
  107.9 2.9 %shard_map.41 = (s16[50,32,128]{2,1,0:T(8,128)(2,1)S(1)}, s16[50,32,128]{2,1,0:T(8,128)(2,1)S(1)}, s16[50,32,128]{2,1,0:T(8,128)(2,1)S(1)}, s16[50,32,128]{2,1,0:T(8,128)(2,1)S(1)}) custom-call(s32[3]{0:T(128)S(1)} %pad_add_fusion.1.place_ref, s32[8,128]{1,0:T(8,128)S(1)} %concatenate.8.want_ref, s16[66,32,128]{2,1,0:T(8,128)(2,1)S(1)} %get-tuple-element.33.refs_0_, ...), custom_call_target="tpu_custom_call" | custom-call | tf_op jit(solution)/shard_map/pallas_call | solution.py:338
  110.8 0.1 collective-permute-start.21
  110.9 6.3 %collective-permute-start.22 = (s16[50,32,128]{2,1,0:T(8,128)(2,1)S(1)}, s16[50,32,128]{2,1,0:T(8,128)(2,1)S(1)}, u32[]{:S(2)}, u32[]{:S(2)}) collective-permute-start(s16[50,32,128]{2,1,0:T(8,128)(2,1)S(1)} %get-tuple-element.43), channel_id=1, source_target_pairs={{0,128},{1,5},{2,130},{3,7},{4,132},{5,1},{6,134},{7,3},{8,136},{9... | collective-permute-start | bytes 1228808 | tf_op jit(solution)/shard_map/ppermute | solution.py:70
  117.2 0.8 collective-permute-start.23
  117.9 0.1 collective-permute-done.21.refs_1_
  118.0 4.6 %collective-permute-done.22.refs_2_ = s16[50,32,128]{2,1,0:T(8,128)(2,1)S(1)} collective-permute-done((s16[50,32,128]{2,1,0:T(8,128)(2,1)S(1)}, s16[50,32,128]{2,1,0:T(8,128)(2,1)S(1)}, u32[]{:S(2)}, u32[]{:S(2)}) %collective-permute-start.22) | collective-permute-done | bytes 409632 | tf_op jit(solution)/shard_map/ppermute | solution.py:70
  122.6 4.3 %collective-permute-done.23.refs_3_ = s16[50,32,128]{2,1,0:T(8,128)(2,1)S(1)} collective-permute-done((s16[50,32,128]{2,1,0:T(8,128)(2,1)S(1)}, s16[50,32,128]{2,1,0:T(8,128)(2,1)S(1)}, u32[]{:S(2)}, u32[]{:S(2)}) %collective-permute-start.23) | collective-permute-done | bytes 409632 | tf_op jit(solution)/shard_map/ppermute | solution.py:70
  126.9 0.7 shard_map.42
  127.6 17.8 %all_to_all.10.pieces = s16[16,7,16,128]{3,2,1,0:T(8,128)(2,1)S(1)} all-to-all(s16[16,7,16,128]{3,2,1,0:T(8,128)(2,1)S(1)} %shard_map.42), channel_id=1, replica_groups=mesh['x'=4,'z'=8,'y'=4,'core'=2] {'z','core'}, dimensions={0} | all-to-all | bytes 917504 | tf_op jit(solution)/shard_map/all_to_all | solution.py:27
  145.4 0.8 shard_map.43
  (4 shorter events, 0.1 us)
Async XLA Ops:
  1.6 24.5 %all-to-all-start = ((bf16[16,3,16,256]{3,2,1,0:T(8,128)(2,1)}), bf16[16,3,16,256]{3,2,1,0:T(8,128)(2,1)S(1)}, u32[]{:S(2)}, u32[]{:S(2)}) async-start(bf16[16,3,16,256]{3,2,1,0:T(8,128)(2,1)} %bitcast.7), calls=%async_computation | async-start | bytes 786432 | tf_op jit(solution)/shard_map/all_to_all | solution.py:27
  26.1 13.9 %collective-permute-start.4 = (bf16[16,3,16,256]{3,2,1,0:T(8,128)(2,1)S(1)}, bf16[16,3,16,256]{3,2,1,0:T(8,128)(2,1)S(1)}, u32[]{:S(2)}, u32[]{:S(2)}) collective-permute-start(bf16[16,3,16,256]{3,2,1,0:T(8,128)(2,1)S(1)} %all-to-all-done.refs_0_), channel_id=1, source_target_pairs={{0,64},{1,3},{2,66},{3,5},{4,68},{5,7},{6,70},{7,1},{8,72},{9,11},... | collective-permute-start | bytes 1179656 | tf_op jit(solution)/shard_map/ppermute | solution.py:70
  27.4 12.6 %collective-permute-start.5 = (bf16[16,3,16,256]{3,2,1,0:T(8,128)(2,1)S(1)}, bf16[16,3,16,256]{3,2,1,0:T(8,128)(2,1)S(1)}, u32[]{:S(2)}, u32[]{:S(2)}) collective-permute-start(bf16[16,3,16,256]{3,2,1,0:T(8,128)(2,1)S(1)} %all-to-all-done.refs_0_), channel_id=1, source_target_pairs={{0,128},{1,5},{2,130},{3,7},{4,132},{5,1},{6,134},{7,3},{8,136},{9... | collective-permute-start | bytes 1179656 | tf_op jit(solution)/shard_map/ppermute | solution.py:70
  30.0 10.0 %collective-permute-start.6 = (bf16[16,3,16,256]{3,2,1,0:T(8,128)(2,1)S(1)}, bf16[16,3,16,256]{3,2,1,0:T(8,128)(2,1)S(1)}, u32[]{:S(2)}, u32[]{:S(2)}) collective-permute-start(bf16[16,3,16,256]{3,2,1,0:T(8,128)(2,1)S(1)} %all-to-all-done.refs_0_), channel_id=1, source_target_pairs={{0,192},{1,7},{2,194},{3,1},{4,196},{5,3},{6,198},{7,5},{8,200},{9... | collective-permute-start | bytes 1179656 | tf_op jit(solution)/shard_map/ppermute | solution.py:70
  31.2 1.2 collective-permute-start
  32.4 3.2 %collective-permute-start.1 = (s32[2,128]{1,0:T(2,128)S(1)}, s32[2,128]{1,0:T(2,128)S(1)}, u32[]{:S(2)}, u32[]{:S(2)}) collective-permute-start(s32[2,128]{1,0:T(2,128)S(1)} %pad_add_fusion), channel_id=1, source_target_pairs={{0,6},{1,193},{2,0},{3,195},{4,2},{5,197},{6,4},{7,199},{8,14},{9,... | collective-permute-start | bytes 3080 | tf_op jit(solution)/shard_map/ppermute | solution.py:70
  34.9 4.2 %collective-permute-start.2 = (s32[2,128]{1,0:T(2,128)S(1)}, s32[2,128]{1,0:T(2,128)S(1)}, u32[]{:S(2)}, u32[]{:S(2)}) collective-permute-start(s32[2,128]{1,0:T(2,128)S(1)} %pad_add_fusion), channel_id=1, source_target_pairs={{0,4},{1,129},{2,6},{3,131},{4,0},{5,133},{6,2},{7,135},{8,12},{9,... | collective-permute-start | bytes 3080 | tf_op jit(solution)/shard_map/ppermute | solution.py:70
  35.6 4.4 %collective-permute-start.3 = (s32[2,128]{1,0:T(2,128)S(1)}, s32[2,128]{1,0:T(2,128)S(1)}, u32[]{:S(2)}, u32[]{:S(2)}) collective-permute-start(s32[2,128]{1,0:T(2,128)S(1)} %pad_add_fusion), channel_id=1, source_target_pairs={{0,2},{1,65},{2,4},{3,67},{4,6},{5,69},{6,0},{7,71},{8,10},{9,73},... | collective-permute-start | bytes 3080 | tf_op jit(solution)/shard_map/ppermute | solution.py:70
  41.2 9.6 %collective-permute-start.11 = (bf16[32,32,256]{2,1,0:T(8,128)(2,1)S(1)}, bf16[32,32,256]{2,1,0:T(8,128)(2,1)S(1)}, u32[]{:S(2)}, u32[]{:S(2)}) collective-permute-start(bf16[32,32,256]{2,1,0:T(8,128)(2,1)S(1)} %get-tuple-element.30), channel_id=1, source_target_pairs={{0,2},{1,65},{2,4},{3,67},{4,6},{5,69},{6,0},{7,71},{8,10},{9,73},... | collective-permute-start | bytes 1572872 | tf_op jit(solution)/shard_map/ppermute | solution.py:70
  41.8 14.9 %collective-permute-start.12 = (bf16[32,32,256]{2,1,0:T(8,128)(2,1)S(1)}, bf16[32,32,256]{2,1,0:T(8,128)(2,1)S(1)}, u32[]{:S(2)}, u32[]{:S(2)}) collective-permute-start(bf16[32,32,256]{2,1,0:T(8,128)(2,1)S(1)} %get-tuple-element.31), channel_id=1, source_target_pairs={{0,4},{1,129},{2,6},{3,131},{4,0},{5,133},{6,2},{7,135},{8,12},{9,... | collective-permute-start | bytes 1572872 | tf_op jit(solution)/shard_map/ppermute | solution.py:70
  44.3 16.7 %collective-permute-start.13 = (bf16[32,32,256]{2,1,0:T(8,128)(2,1)S(1)}, bf16[32,32,256]{2,1,0:T(8,128)(2,1)S(1)}, u32[]{:S(2)}, u32[]{:S(2)}) collective-permute-start(bf16[32,32,256]{2,1,0:T(8,128)(2,1)S(1)} %get-tuple-element.32), channel_id=1, source_target_pairs={{0,6},{1,193},{2,0},{3,195},{4,2},{5,197},{6,4},{7,199},{8,14},{9,... | collective-permute-start | bytes 1572872 | tf_op jit(solution)/shard_map/ppermute | solution.py:70
  45.4 23.4 %collective-permute-start.10 = (bf16[32,32,256]{2,1,0:T(8,128)(2,1)S(1)}, bf16[32,32,256]{2,1,0:T(8,128)(2,1)S(1)}, u32[]{:S(2)}, u32[]{:S(2)}) collective-permute-start(bf16[32,32,256]{2,1,0:T(8,128)(2,1)S(1)} %get-tuple-element.28), channel_id=1, source_target_pairs={{0,7},{1,192},{2,1},{3,194},{4,3},{5,196},{6,5},{7,198},{8,15},{9,... | collective-permute-start | bytes 1572872 | tf_op jit(solution)/shard_map/ppermute | solution.py:70
  48.7 20.1 %collective-permute-start.7 = (bf16[32,32,256]{2,1,0:T(8,128)(2,1)S(1)}, bf16[32,32,256]{2,1,0:T(8,128)(2,1)S(1)}, u32[]{:S(2)}, u32[]{:S(2)}) collective-permute-start(bf16[32,32,256]{2,1,0:T(8,128)(2,1)S(1)} %get-tuple-element.25), channel_id=1, source_target_pairs={{0,1},{1,0},{2,3},{3,2},{4,5},{5,4},{6,7},{7,6},{8,9},{9,8},{10,11... | collective-permute-start | bytes 1572872 | tf_op jit(solution)/shard_map/ppermute | solution.py:74
  50.8 18.0 %collective-permute-start.8 = (bf16[32,32,256]{2,1,0:T(8,128)(2,1)S(1)}, bf16[32,32,256]{2,1,0:T(8,128)(2,1)S(1)}, u32[]{:S(2)}, u32[]{:S(2)}) collective-permute-start(bf16[32,32,256]{2,1,0:T(8,128)(2,1)S(1)} %get-tuple-element.26), channel_id=1, source_target_pairs={{0,3},{1,64},{2,5},{3,66},{4,7},{5,68},{6,1},{7,70},{8,11},{9,72},... | collective-permute-start | bytes 1572872 | tf_op jit(solution)/shard_map/ppermute | solution.py:70
  56.7 13.4 %collective-permute-start.9 = (bf16[32,32,256]{2,1,0:T(8,128)(2,1)S(1)}, bf16[32,32,256]{2,1,0:T(8,128)(2,1)S(1)}, u32[]{:S(2)}, u32[]{:S(2)}) collective-permute-start(bf16[32,32,256]{2,1,0:T(8,128)(2,1)S(1)} %get-tuple-element.27), channel_id=1, source_target_pairs={{0,5},{1,128},{2,7},{3,130},{4,1},{5,132},{6,3},{7,134},{8,13},{9,... | collective-permute-start | bytes 1572872 | tf_op jit(solution)/shard_map/ppermute | solution.py:70
  75.6 12.5 %collective-permute-start.17 = (s16[66,32,128]{2,1,0:T(8,128)(2,1)S(1)}, s16[66,32,128]{2,1,0:T(8,128)(2,1)S(1)}, u32[]{:S(2)}, u32[]{:S(2)}) collective-permute-start(s16[66,32,128]{2,1,0:T(8,128)(2,1)S(1)} %get-tuple-element.37), channel_id=1, source_target_pairs={{0,1},{1,0},{2,3},{3,2},{4,5},{5,4},{6,7},{7,6},{8,9},{9,8},{10,11... | collective-permute-start | bytes 1622024 | tf_op jit(solution)/shard_map/ppermute | solution.py:74
  80.3 10.3 %collective-permute-start.18 = (s16[66,32,128]{2,1,0:T(8,128)(2,1)S(1)}, s16[66,32,128]{2,1,0:T(8,128)(2,1)S(1)}, u32[]{:S(2)}, u32[]{:S(2)}) collective-permute-start(s16[66,32,128]{2,1,0:T(8,128)(2,1)S(1)} %get-tuple-element.38), channel_id=1, source_target_pairs={{0,193},{1,6},{2,195},{3,0},{4,197},{5,2},{6,199},{7,4},{8,201},{9... | collective-permute-start | bytes 1622024 | tf_op jit(solution)/shard_map/ppermute | solution.py:70
  80.3 11.1 %collective-permute-start.19 = (s16[66,32,128]{2,1,0:T(8,128)(2,1)S(1)}, s16[66,32,128]{2,1,0:T(8,128)(2,1)S(1)}, u32[]{:S(2)}, u32[]{:S(2)}) collective-permute-start(s16[66,32,128]{2,1,0:T(8,128)(2,1)S(1)} %get-tuple-element.39), channel_id=1, source_target_pairs={{0,129},{1,4},{2,131},{3,6},{4,133},{5,0},{6,135},{7,2},{8,137},{9... | collective-permute-start | bytes 1622024 | tf_op jit(solution)/shard_map/ppermute | solution.py:70
  82.1 23.4 %collective-permute-start.20 = (s16[66,32,128]{2,1,0:T(8,128)(2,1)S(1)}, s16[66,32,128]{2,1,0:T(8,128)(2,1)S(1)}, u32[]{:S(2)}, u32[]{:S(2)}) collective-permute-start(s16[66,32,128]{2,1,0:T(8,128)(2,1)S(1)} %get-tuple-element.40), channel_id=1, source_target_pairs={{0,65},{1,2},{2,67},{3,4},{4,69},{5,6},{6,71},{7,0},{8,73},{9,10},... | collective-permute-start | bytes 1622024 | tf_op jit(solution)/shard_map/ppermute | solution.py:70
  88.0 17.6 %collective-permute-start.14 = (s16[66,32,128]{2,1,0:T(8,128)(2,1)S(1)}, s16[66,32,128]{2,1,0:T(8,128)(2,1)S(1)}, u32[]{:S(2)}, u32[]{:S(2)}) collective-permute-start(s16[66,32,128]{2,1,0:T(8,128)(2,1)S(1)} %get-tuple-element.34), channel_id=1, source_target_pairs={{0,6},{1,193},{2,0},{3,195},{4,2},{5,197},{6,4},{7,199},{8,14},{9,... | collective-permute-start | bytes 1622024 | tf_op jit(solution)/shard_map/ppermute | solution.py:70
  88.2 17.4 %collective-permute-start.15 = (s16[66,32,128]{2,1,0:T(8,128)(2,1)S(1)}, s16[66,32,128]{2,1,0:T(8,128)(2,1)S(1)}, u32[]{:S(2)}, u32[]{:S(2)}) collective-permute-start(s16[66,32,128]{2,1,0:T(8,128)(2,1)S(1)} %get-tuple-element.35), channel_id=1, source_target_pairs={{0,4},{1,129},{2,6},{3,131},{4,0},{5,133},{6,2},{7,135},{8,12},{9,... | collective-permute-start | bytes 1622024 | tf_op jit(solution)/shard_map/ppermute | solution.py:70
  90.6 17.4 %collective-permute-start.16 = (s16[66,32,128]{2,1,0:T(8,128)(2,1)S(1)}, s16[66,32,128]{2,1,0:T(8,128)(2,1)S(1)}, u32[]{:S(2)}, u32[]{:S(2)}) collective-permute-start(s16[66,32,128]{2,1,0:T(8,128)(2,1)S(1)} %get-tuple-element.36), channel_id=1, source_target_pairs={{0,2},{1,65},{2,4},{3,67},{4,6},{5,69},{6,0},{7,71},{8,10},{9,73},... | collective-permute-start | bytes 1622024 | tf_op jit(solution)/shard_map/ppermute | solution.py:70
  110.8 7.2 %collective-permute-start.21 = (s16[50,32,128]{2,1,0:T(8,128)(2,1)S(1)}, s16[50,32,128]{2,1,0:T(8,128)(2,1)S(1)}, u32[]{:S(2)}, u32[]{:S(2)}) collective-permute-start(s16[50,32,128]{2,1,0:T(8,128)(2,1)S(1)} %get-tuple-element.42), channel_id=1, source_target_pairs={{0,192},{1,7},{2,194},{3,1},{4,196},{5,3},{6,198},{7,5},{8,200},{9... | collective-permute-start | bytes 1228808 | tf_op jit(solution)/shard_map/ppermute | solution.py:70
  110.9 11.7 %collective-permute-start.22 = (s16[50,32,128]{2,1,0:T(8,128)(2,1)S(1)}, s16[50,32,128]{2,1,0:T(8,128)(2,1)S(1)}, u32[]{:S(2)}, u32[]{:S(2)}) collective-permute-start(s16[50,32,128]{2,1,0:T(8,128)(2,1)S(1)} %get-tuple-element.43), channel_id=1, source_target_pairs={{0,128},{1,5},{2,130},{3,7},{4,132},{5,1},{6,134},{7,3},{8,136},{9... | collective-permute-start | bytes 1228808 | tf_op jit(solution)/shard_map/ppermute | solution.py:70
  117.2 9.7 %collective-permute-start.23 = (s16[50,32,128]{2,1,0:T(8,128)(2,1)S(1)}, s16[50,32,128]{2,1,0:T(8,128)(2,1)S(1)}, u32[]{:S(2)}, u32[]{:S(2)}) collective-permute-start(s16[50,32,128]{2,1,0:T(8,128)(2,1)S(1)} %get-tuple-element.44), channel_id=1, source_target_pairs={{0,64},{1,3},{2,66},{3,5},{4,68},{5,7},{6,70},{7,1},{8,72},{9,11},... | collective-permute-start | bytes 1228808 | tf_op jit(solution)/shard_map/ppermute | solution.py:70
